TPU v7x, 256 devices: a whole 4x4x8 slice. The times are simulated.
256 devices in a mesh: dp: 64 (over z, y, core), mp: 4 (over x).
Axes of the slice: x: 4, y: 4, z: 8, core: 2. Of those that a mesh axis runs over, the one named last changes fastest.
Arguments:
- tokens: bfloat16 [128, 6656], P('dp', 'mp'), may hold values from -6 to 6
- grad_out: bfloat16 [128, 6656], P('dp', 'mp'), may hold values from -1.5 to 1.5
- gate_src: bfloat16 [10240, 6656], P(('dp', 'mp')), may hold values from -0.078125 to 0.078125
- up_src: bfloat16 [10240, 6656], P(('dp', 'mp')), may hold values from -0.078125 to 0.078125
- down_src: bfloat16 [10240, 6656], P(('dp', 'mp')), may hold values from -0.25 to 0.25
- unit_map: int32 [15360], P(('dp', 'mp')), may hold values from 0 to 10239, as said below
- copy_flag: int32 [15360], P(('dp', 'mp')), may hold values from 0 to 1, as said below
Outputs:
- layer_out: bfloat16 [128, 6656], P('dp', 'mp')
- grad_tokens: bfloat16 [128, 6656], P('dp', 'mp')
- grad_gate: bfloat16 [15360, 6656], P(('dp', 'mp'))
- grad_up: bfloat16 [15360, 6656], P(('dp', 'mp'))
- grad_down: bfloat16 [15360, 6656], P(('dp', 'mp'))
Inputs may be any that keep to these rules, and one draw needn't show every extreme that they name: `unit_map`: the widened unit j lies on the device of flat index j // 60 along dp+mp, and its source unit lies on a device with the same mp index. Every source unit is the source of one or two widened units. For every pair of devices, at most 3 widened units of the one have their source on the other; every device takes exactly 3 from some device and gives exactly 3 to some device. `copy_flag`: A source unit with one widened unit gives it flag 1; of a source's two widened units at least one has flag 1.
All inputs are finite; a program needn't handle non-finite values.
Results may differ from a plain program's by a relative error of at most 0.0049.
Values may be sent and summed in bfloat16 or wider, within the bound.
A program may use at most 128 MiB of HBM per device.

v0:
```python
import jax
import jax.numpy as jnp
from jax import lax
from jax.sharding import PartitionSpec as P


def layer_pass(inputs, cotangent, gate_rows, up_rows, down_rows):
    dims = (((1,), (1,)), ((), ()))
    pre_gate = lax.dot_general(inputs, gate_rows, dims, preferred_element_type=jnp.float32)
    pre_up = lax.dot_general(inputs, up_rows, dims, preferred_element_type=jnp.float32)
    sigma = jax.nn.sigmoid(pre_gate)
    active = pre_gate * sigma
    hidden = (active * pre_up).astype(jnp.bfloat16)
    out_part = jnp.dot(hidden, down_rows, preferred_element_type=jnp.float32)
    grad_hidden = lax.dot_general(cotangent, down_rows, dims, preferred_element_type=jnp.float32)
    grad_pre_gate = (grad_hidden * pre_up * (sigma + active * (1.0 - sigma))).astype(jnp.bfloat16)
    grad_pre_up = (grad_hidden * active).astype(jnp.bfloat16)
    input_part = jnp.dot(grad_pre_gate, gate_rows, preferred_element_type=jnp.float32)
    input_part = input_part + jnp.dot(grad_pre_up, up_rows, preferred_element_type=jnp.float32)
    tdims = (((0,), (0,)), ((), ()))
    gate_grad = lax.dot_general(
        grad_pre_gate, inputs, tdims, preferred_element_type=jnp.float32
    ).astype(jnp.bfloat16)
    up_grad = lax.dot_general(
        grad_pre_up, inputs, tdims, preferred_element_type=jnp.float32
    ).astype(jnp.bfloat16)
    down_grad = lax.dot_general(
        hidden, cotangent, tdims, preferred_element_type=jnp.float32
    ).astype(jnp.bfloat16)
    return (out_part, input_part, gate_grad, up_grad, down_grad)


def per_device(tokens, grad_out, gate_src, up_src, down_src, unit_map, copy_flag):
    n_dp = lax.axis_size("dp")
    n_mp = lax.axis_size("mp")
    src_dev = gate_src.shape[0]
    wide_dev = unit_map.shape[0]
    quant = (wide_dev + 3 * n_dp - 1) // (3 * n_dp)
    slots = 3 * quant
    my_mp = lax.axis_index("mp")
    my_flat = lax.axis_index("dp") * n_mp + my_mp
    unit_code = (unit_map * 2 + copy_flag).reshape(-1, 2)
    packed = unit_code[:, 0] + unit_code[:, 1] * 32768
    full_packed = lax.all_gather(packed, ("dp", "mp"), axis=0, tiled=True)
    lower_half = full_packed % 32768
    upper_half = full_packed // 32768
    full_code = jnp.stack([lower_half, upper_half], axis=1).reshape(-1)
    full_map = full_code // 2
    full_flag = full_code % 2
    share = jax.ops.segment_sum(
        full_flag.astype(jnp.float32), full_map, num_segments=src_dev * n_dp * n_mp
    )
    scale = copy_flag.astype(jnp.float32) / share[unit_map]
    owner_dp = unit_map // src_dev // n_mp
    unit_index = jnp.arange(wide_dev, dtype=jnp.int32)
    same_owner = (owner_dp[:, None] == owner_dp[None, :]) & (
        unit_index[:, None] > unit_index[None, :]
    )
    arrival = jnp.sum(same_owner.astype(jnp.int32), axis=1)
    recv_row = owner_dp * slots + arrival
    requests = lax.dynamic_index_in_dim(
        full_map.reshape(n_dp, n_mp, wide_dev), my_mp, 1, keepdims=False
    )
    owned = requests // src_dev == my_flat
    rank = jnp.cumsum(owned.astype(jnp.int32), axis=1) - 1
    slot_ids = jnp.arange(slots, dtype=jnp.int32)
    placed = owned[:, None, :] & (rank[:, None, :] == slot_ids[None, :, None])
    local = requests - my_flat * src_dev
    send_idx = jnp.sum(jnp.where(placed, local[:, None, :], 0), axis=2).reshape(-1)
    tok_feat, cot_feat = (
        lax.all_gather(tokens, "mp", axis=1, tiled=True),
        lax.all_gather(grad_out, "mp", axis=1, tiled=True),
    )
    inputs, cotangent = (
        lax.all_gather(tok_feat, "dp", axis=0, tiled=True),
        lax.all_gather(cot_feat, "dp", axis=0, tiled=True),
    )
    moved_gate, moved_up, moved_down = (
        lax.all_to_all(gate_src[send_idx], "dp", split_axis=0, concat_axis=0, tiled=True),
        lax.all_to_all(up_src[send_idx], "dp", split_axis=0, concat_axis=0, tiled=True),
        lax.all_to_all(down_src[send_idx], "dp", split_axis=0, concat_axis=0, tiled=True),
    )
    gate_wide = moved_gate[recv_row]
    up_wide = moved_up[recv_row]
    down_wide = (moved_down[recv_row].astype(jnp.float32) * scale[:, None]).astype(jnp.bfloat16)
    out_part, input_part, grad_gate, grad_up, grad_down = layer_pass(
        inputs, cotangent, gate_wide, up_wide, down_wide
    )
    out_cols, input_cols = (
        lax.psum_scatter(out_part, "mp", scatter_dimension=1, tiled=True),
        lax.psum_scatter(input_part, "mp", scatter_dimension=1, tiled=True),
    )
    out_sum, input_sum = (
        lax.psum_scatter(out_cols, "dp", scatter_dimension=0, tiled=True),
        lax.psum_scatter(input_cols, "dp", scatter_dimension=0, tiled=True),
    )
    return (
        out_sum.astype(jnp.bfloat16),
        input_sum.astype(jnp.bfloat16),
        grad_gate,
        grad_up,
        grad_down,
    )


def solution(mesh):
    in_specs = (
        P("dp", "mp"),
        P("dp", "mp"),
        P(("dp", "mp"), None),
        P(("dp", "mp"), None),
        P(("dp", "mp"), None),
        P(("dp", "mp")),
        P(("dp", "mp")),
    )
    out_specs = (
        P("dp", "mp"),
        P("dp", "mp"),
        P(("dp", "mp"), None),
        P(("dp", "mp"), None),
        P(("dp", "mp"), None),
    )
    return jax.shard_map(
        per_device, mesh=mesh, in_specs=in_specs, out_specs=out_specs, check_vma=False
    )
```

profile of v0, /device:TPU:2, one launch (start us, length us, event | category | flops | bytes accessed | tf_op | source)
XLA Modules:
  0.0 798.3 jit_solution(5214602645316661995)
XLA Ops:
  8.5 78.8 %all-reduce = s32[7680]{0:T(1024)S(1)} all-reduce(s32[7680]{0:T(1024)S(1)} %dynamic-update-slice), channel_id=2, replica_groups=mesh['dp'=64,'mp'=4] {'dp','mp'}, use_global_device_ids=true, to_apply=%add | all-reduce | flops 7680 | bytes 61440 | tf_op jit(solution)/shard_map/all_gather | solution.py:44
  96.1 4.0 all_to_all.30
  100.1 7.7 all-to-all-start.2
  109.9 4.0 all_to_all.27
  113.9 73.3 %all-to-all-done.2 = bf16[64,3,6656]{2,1,0:T(4,128)(2,1)} async-done(((bf16[64,3,6656]{2,1,0:T(4,128)(2,1)}), bf16[64,3,6656]{2,1,0:T(4,128)(2,1)}, u32[]{:S(2)}, u32[]{:S(2)}) %all-to-all-start.2) | async-done | bytes 2555936 | tf_op jit(solution)/shard_map/all_to_all | solution.py:81
  187.2 5.6 all-to-all-start.1
  192.9 11.4 %all_gather.16 = bf16[2,6656]{1,0:T(2,128)(2,1)} all-gather(bf16[2,1664]{1,0:T(2,128)(2,1)S(1)} %copy-done.8), channel_id=1, replica_groups=mesh['dp'=64,'mp'=4] {'mp'}, dimensions={1}, use_global_device_ids=true | all-gather | bytes 33280 | tf_op jit(solution)/shard_map/all_gather | solution.py:71
  206.5 4.0 all_to_all.24
  210.5 64.6 %all-to-all-done.1 = bf16[64,3,6656]{2,1,0:T(4,128)(2,1)} async-done(((bf16[64,3,6656]{2,1,0:T(4,128)(2,1)}), bf16[64,3,6656]{2,1,0:T(4,128)(2,1)}, u32[]{:S(2)}, u32[]{:S(2)}) %all-to-all-start.1) | async-done | bytes 2555936 | tf_op jit(solution)/shard_map/all_to_all | solution.py:80
  275.1 5.6 all-to-all-start
  280.8 11.4 %all_gather.18 = bf16[2,6656]{1,0:T(2,128)(2,1)} all-gather(bf16[2,1664]{1,0:T(2,128)(2,1)S(1)} %copy-done.9), channel_id=1, replica_groups=mesh['dp'=64,'mp'=4] {'mp'}, dimensions={1}, use_global_device_ids=true | all-gather | bytes 33280 | tf_op jit(solution)/shard_map/all_gather | solution.py:72
  296.3 5.3 reshape.145
  301.9 80.7 %scatter_custom_fusion = f32[10240]{0:T(1024)S(1)} fusion(s32[15360]{0:T(1024)S(1)} %bitcast.37, f32[15360]{0:T(1024)S(1)} %fusion.3, f32[]{:T(128)} %constant.106.clone.1), kind=kCustom, calls=%fused_computation.55 | custom fusion | flops 15360 | bytes 40964 | tf_op jit(solution)/shard_map/scatter-add | solution.py:50
  383.6 3.9 reshape.219
  387.6 4.7 reshape.221
  392.3 6.9 all_to_all.32
  399.2 4.7 gather_fusion.5
  404.0 6.9 all_to_all.29
  410.9 4.7 gather_fusion.3
  415.6 6.9 all_to_all.26
  422.6 3.8 gather_fusion.1
  444.2 32.5 %reduce-scatter.5.cloned.1.call-done = f32[128,1664]{1,0:T(8,128)} async-done(((f32[128,6656]{1,0:T(8,128)}), f32[128,1664]{1,0:T(8,128)}) %reduce-scatter.5.cloned.1.call-update) | async-done | bytes 851984 | tf_op jit(solution)/shard_map/reduce_scatter | solution.py:91
  476.7 45.1 %reduce-scatter.3.cloned.1.call-done = f32[128,1664]{1,0:T(8,128)} async-done(((f32[128,6656]{1,0:T(8,128)}), f32[128,1664]{1,0:T(8,128)}) %reduce-scatter.3.cloned.1.call-update) | async-done | bytes 851984 | tf_op jit(solution)/shard_map/reduce_scatter | solution.py:90
  521.8 269.4 %all-reduce.5 = (bf16[128,1664]{1,0:T(8,128)(2,1)S(1)}, bf16[128,1664]{1,0:T(8,128)(2,1)S(1)}) all-reduce(f32[128,1664]{1,0:T(8,128)} %reduce-scatter.3.cloned.1.call-done, f32[128,1664]{1,0:T(8,128)} %reduce-scatter.5.cloned.1.call-done), channel_id=4, replica_groups=mesh['dp'=64,'mp'=4] {'dp'}, use_global_device_ids=true, to_apply=%region_5.6.clone | all-reduce | flops 425984 | bytes 2555904
  (81 shorter events, 37.2 us)
Async XLA Ops:
  7.2 86.8 %copy-start = (bf16[40,6656]{1,0:T(8,128)(2,1)S(1)}, bf16[40,6656]{1,0:T(8,128)(2,1)}, u32[]{:S(2)}) copy-start(bf16[40,6656]{1,0:T(8,128)(2,1)} %param.11) | copy-start | bytes 1597444
  100.1 7.7 copy-start.2
  100.1 87.1 %all-to-all-start.2 = ((bf16[64,3,6656]{2,1,0:T(4,128)(2,1)}), bf16[64,3,6656]{2,1,0:T(4,128)(2,1)}, u32[]{:S(2)}, u32[]{:S(2)}) async-start(bf16[64,3,6656]{2,1,0:T(4,128)(2,1)} %all_to_all.30), calls=%async_computation.2 | async-start | bytes 6815744 | tf_op jit(solution)/shard_map/all_to_all | solution.py:81
  113.9 79.0 %copy-start.8 = (bf16[2,1664]{1,0:T(2,128)(2,1)S(1)}, bf16[2,1664]{1,0:T(2,128)(2,1)}, u32[]{:S(2)}) copy-start(bf16[2,1664]{1,0:T(2,128)(2,1)} %param.7) | copy-start | bytes 19972
  113.9 90.4 %copy-start.3 = (bf16[40,6656]{1,0:T(8,128)(2,1)S(1)}, bf16[40,6656]{1,0:T(8,128)(2,1)}, u32[]{:S(2)}) copy-start(bf16[40,6656]{1,0:T(8,128)(2,1)} %param.9) | copy-start | bytes 1597444
  187.2 87.9 %all-to-all-start.1 = ((bf16[64,3,6656]{2,1,0:T(4,128)(2,1)}), bf16[64,3,6656]{2,1,0:T(4,128)(2,1)}, u32[]{:S(2)}, u32[]{:S(2)}) async-start(bf16[64,3,6656]{2,1,0:T(4,128)(2,1)} %all_to_all.27), calls=%async_computation.1 | async-start | bytes 6815744 | tf_op jit(solution)/shard_map/all_to_all | solution.py:80
  192.8 190.8 %all-gather.6.cloned.1.call-start = ((), (), s32[]{:S(2)}) async-start(), calls=%async_computation.7 | async-start | bytes 1730560 | tf_op jit(solution)/shard_map/all_gather | solution.py:75
  210.5 70.3 %copy-start.9 = (bf16[2,1664]{1,0:T(2,128)(2,1)S(1)}, bf16[2,1664]{1,0:T(2,128)(2,1)}, u32[]{:S(2)}) copy-start(bf16[2,1664]{1,0:T(2,128)(2,1)} %param.8) | copy-start | bytes 19972
  275.1 140.5 %all-to-all-start = ((bf16[64,3,6656]{2,1,0:T(4,128)(2,1)}), bf16[64,3,6656]{2,1,0:T(4,128)(2,1)}, u32[]{:S(2)}, u32[]{:S(2)}) async-start(bf16[64,3,6656]{2,1,0:T(4,128)(2,1)} %all_to_all.24), calls=%async_computation | async-start | bytes 6815744 | tf_op jit(solution)/shard_map/all_to_all | solution.py:79
  280.8 106.8 %all-gather.8.cloned.1.call-start = ((), (), s32[]{:S(2)}) async-start(), calls=%async_computation.8 | async-start | bytes 1730560 | tf_op jit(solution)/shard_map/all_gather | solution.py:76
  292.3 184.4 %reduce-scatter.5.cloned.1.call-start = ((), (), s32[]{:S(2)}) async-start(), calls=%async_computation.6 | async-start | bytes 4259840 | tf_op jit(solution)/shard_map/reduce_scatter | solution.py:91
  296.3 87.3 %copy-start.10 = (s32[60]{0:T(128)S(1)}, s32[60]{0:T(128)}, u32[]{:S(2)}) copy-start(s32[60]{0:T(128)} %param.13) | copy-start | bytes 724
  426.4 2.7 copy-start.4
  426.4 2.7 copy-start.5
  429.9 1.2 copy-start.7
  433.4 1.2 copy-start.6
  433.4 88.4 %reduce-scatter.3.cloned.1.call-start = ((), (), s32[]{:S(2)}) async-start(), calls=%async_computation.5 | async-start | bytes 4259840 | tf_op jit(solution)/shard_map/reduce_scatter | solution.py:90
  437.0 0.7 copy-start.11
  441.6 350.2 %copy-start.1 = (bf16[40,6656]{1,0:T(8,128)(2,1)S(1)}, bf16[40,6656]{1,0:T(8,128)(2,1)}, u32[]{:S(2)}) copy-start(bf16[40,6656]{1,0:T(8,128)(2,1)} %param.11) | copy-start | bytes 1597444
Sparse Core Ops, SparseCore 0:
  204.5 84.0 all-gather.5
  292.4 84.0 all-gather.7
  433.5 43.0 reduce-scatter.4
  479.1 42.6 reduce-scatter.2
where the time goes:
time: 800 us; the launch traced here: 798 us
  blocking collectives  371 us (46%)
  waiting for transfers between devices  216 us (27%)
  other arithmetic  83.1 us (10%)
  local copies, waits for them, and re-layouts  80.3 us (10%)
  starting transfers between devices  19.3 us (2%)
  between operations  14.9 us (2%)
  matrix products  14.1 us (2%)
    unnamed x1, blocking collectives  269 us
    scatter-add x1, other arithmetic, per_device(): jax.ops.segment_sum(full_flag.astype(jnp.float32), full_map, num_segments...  80.7 us
    all_gather x1, blocking collectives, per_device(): full_packed = lax.all_gather(packed, ('dp', 'mp'), axis=0, tiled=True)  78.8 us
    all_to_all x1, waiting for transfers between devices, per_device(): lax.all_to_all(down_src[send_idx], 'dp', split_axis=0, concat_axis=0, til...  73.3 us
    all_to_all x1, waiting for transfers between devices, per_device(): lax.all_to_all(up_src[send_idx], 'dp', split_axis=0, concat_axis=0, tiled...  64.6 us
    reduce_scatter x1, waiting for transfers between devices, per_device(): lax.psum_scatter(out_part, 'mp', scatter_dimension=1, tiled=True)  45.1 us
    reduce_scatter x1, waiting for transfers between devices, per_device(): lax.psum_scatter(input_part, 'mp', scatter_dimension=1, tiled=True)  32.5 us
  transfers between devices with their start and end apart: 7, of which 4 were waited for; matrix products, arithmetic and copies ran while one was open for 15% of the time, Pallas kernels for 0%

commit v1 on v0

--- a/solution.py
+++ b/solution.py
@@ -41,7 +41,10 @@
     my_flat = lax.axis_index("dp") * n_mp + my_mp
     unit_code = (unit_map * 2 + copy_flag).reshape(-1, 2)
     packed = unit_code[:, 0] + unit_code[:, 1] * 32768
-    full_packed = lax.all_gather(packed, ("dp", "mp"), axis=0, tiled=True)
+    full_packed = jnp.concatenate(
+        lax.all_to_all(jnp.stack([packed] * lax.axis_size(("dp", "mp"))), ("dp", "mp"), 0, 0),
+        axis=0,
+    )
     lower_half = full_packed % 32768
     upper_half = full_packed // 32768
     full_code = jnp.stack([lower_half, upper_half], axis=1).reshape(-1)

time: 800 us -> 748 us (0.935)
  blocking collectives: 371 us -> 295 us
  starting transfers between devices: 19.3 us -> 32.1 us
  waiting for transfers between devices: 216 us -> 225 us
    all_gather x1 -> x0, blocking collectives: 78.8 us -> none  [per_device(): full_packed = lax.all_gather(packed, ('dp', 'mp'), axis=0, tiled=True)]
    all_to_all x0 -> x1, starting transfers between devices: none -> 14.7 us  [per_device(): lax.all_to_all(jnp.stack([packed] * lax.axis_size(('dp', 'mp'))), ('dp',...]
    all_to_all x0 -> x1, waiting for transfers between devices: none -> 11.3 us  [per_device(): lax.all_to_all(jnp.stack([packed] * lax.axis_size(('dp', 'mp'))), ('dp',...]
  transfers between devices with their start and end apart: 7 -> 8, of which waited for: 4 -> 5; matrix products, arithmetic and copies ran while one was open for 15% -> 16% of each run, Pallas kernels for 0% -> 0%
where the time goes in v1:
time: 748 us; the launch traced here: 746 us
  blocking collectives  295 us (39%)
  waiting for transfers between devices  225 us (30%)
  other arithmetic  84.2 us (11%)
  local copies, waits for them, and re-layouts  81.2 us (11%)
  starting transfers between devices  32.1 us (4%)
  between operations  14.8 us (2%)
  matrix products  14.1 us (2%)
    unnamed x1, blocking collectives  269 us
    scatter-add x1, other arithmetic, per_device(): jax.ops.segment_sum(full_flag.astype(jnp.float32), full_map, num_segments...  80.7 us
    all_to_all x1, waiting for transfers between devices, per_device(): lax.all_to_all(down_src[send_idx], 'dp', split_axis=0, concat_axis=0, til...  73.3 us
    all_to_all x1, waiting for transfers between devices, per_device(): lax.all_to_all(up_src[send_idx], 'dp', split_axis=0, concat_axis=0, tiled...  62.9 us
    reduce_scatter x1, waiting for transfers between devices, per_device(): lax.psum_scatter(out_part, 'mp', scatter_dimension=1, tiled=True)  45.1 us
    reduce_scatter x1, waiting for transfers between devices, per_device(): lax.psum_scatter(input_part, 'mp', scatter_dimension=1, tiled=True)  32.5 us
  transfers between devices with their start and end apart: 8, of which 5 were waited for; matrix products, arithmetic and copies ran while one was open for 16% of the time, Pallas kernels for 0%

profile of v1, /device:TPU:2, one launch (start us, length us, event | category | flops | bytes accessed | tf_op | source)
XLA Modules:
  0.0 746.2 jit_solution(41496251250129796)
XLA Ops:
  9.0 14.7 %all-to-all-start = ((s32[256,1,30]{2,1,0:T(1,128)}), s32[256,1,30]{2,1,0:T(1,128)S(1)}, u32[]{:S(2)}, u32[]{:S(2)}) async-start(s32[256,1,30]{2,1,0:T(1,128)} %stack.4), calls=%async_computation | async-start | bytes 262144 | tf_op jit(solution)/shard_map/all_to_all | solution.py:45
  23.7 11.3 %all-to-all-done = s32[256,1,30]{2,1,0:T(1,128)S(1)} async-done(((s32[256,1,30]{2,1,0:T(1,128)}), s32[256,1,30]{2,1,0:T(1,128)S(1)}, u32[]{:S(2)}, u32[]{:S(2)}) %all-to-all-start) | async-done | bytes 30752 | tf_op jit(solution)/shard_map/all_to_all | solution.py:45
  45.5 4.0 all_to_all.35
  49.5 5.7 all-to-all-start.3
  57.3 4.0 all_to_all.32
  61.3 73.3 %all-to-all-done.3 = bf16[64,3,6656]{2,1,0:T(4,128)(2,1)} async-done(((bf16[64,3,6656]{2,1,0:T(4,128)(2,1)}), bf16[64,3,6656]{2,1,0:T(4,128)(2,1)}, u32[]{:S(2)}, u32[]{:S(2)}) %all-to-all-start.3) | async-done | bytes 2555936 | tf_op jit(solution)/shard_map/all_to_all | solution.py:84
  134.6 5.6 all-to-all-start.2
  140.3 12.6 %all_gather.12 = bf16[2,6656]{1,0:T(2,128)(2,1)} all-gather(bf16[2,1664]{1,0:T(2,128)(2,1)S(1)} %copy-done.8), channel_id=1, replica_groups=mesh['dp'=64,'mp'=4] {'mp'}, dimensions={1}, use_global_device_ids=true | all-gather | bytes 33280 | tf_op jit(solution)/shard_map/all_gather | solution.py:74
  155.0 4.0 all_to_all.29
  159.0 62.9 %all-to-all-done.2 = bf16[64,3,6656]{2,1,0:T(4,128)(2,1)} async-done(((bf16[64,3,6656]{2,1,0:T(4,128)(2,1)}), bf16[64,3,6656]{2,1,0:T(4,128)(2,1)}, u32[]{:S(2)}, u32[]{:S(2)}) %all-to-all-start.2) | async-done | bytes 2555936 | tf_op jit(solution)/shard_map/all_to_all | solution.py:83
  221.9 5.9 all-to-all-start.1
  227.9 12.5 %all_gather.14 = bf16[2,6656]{1,0:T(2,128)(2,1)} all-gather(bf16[2,1664]{1,0:T(2,128)(2,1)S(1)} %copy-done.9), channel_id=1, replica_groups=mesh['dp'=64,'mp'=4] {'mp'}, dimensions={1}, use_global_device_ids=true | all-gather | bytes 33280 | tf_op jit(solution)/shard_map/all_gather | solution.py:75
  244.5 5.3 reshape.262
  250.1 80.7 %scatter_custom_fusion = f32[10240]{0:T(1024)S(1)} fusion(s32[15360]{0:T(1024)S(1)} %bitcast.37, f32[15360]{0:T(1024)S(1)} %fusion.3, f32[]{:T(128)} %constant.106.clone.1), kind=kCustom, calls=%fused_computation.52 | custom fusion | flops 15360 | bytes 40964 | tf_op jit(solution)/shard_map/scatter-add | solution.py:53
  331.6 3.9 reshape.333
  335.5 4.7 reshape.335
  340.3 6.9 all_to_all.37
  347.2 4.7 gather_fusion.5
  351.9 6.9 all_to_all.34
  358.8 4.7 gather_fusion.3
  363.6 6.9 all_to_all.31
  392.1 32.5 %reduce-scatter.5.cloned.1.call-done = f32[128,1664]{1,0:T(8,128)} async-done(((f32[128,6656]{1,0:T(8,128)}), f32[128,1664]{1,0:T(8,128)}) %reduce-scatter.5.cloned.1.call-update) | async-done | bytes 851984 | tf_op jit(solution)/shard_map/reduce_scatter | solution.py:94
  424.6 45.1 %reduce-scatter.3.cloned.1.call-done = f32[128,1664]{1,0:T(8,128)} async-done(((f32[128,6656]{1,0:T(8,128)}), f32[128,1664]{1,0:T(8,128)}) %reduce-scatter.3.cloned.1.call-update) | async-done | bytes 851984 | tf_op jit(solution)/shard_map/reduce_scatter | solution.py:93
  469.7 269.3 %all-reduce.4 = (bf16[128,1664]{1,0:T(8,128)(2,1)S(1)}, bf16[128,1664]{1,0:T(8,128)(2,1)S(1)}) all-reduce(f32[128,1664]{1,0:T(8,128)} %reduce-scatter.3.cloned.1.call-done, f32[128,1664]{1,0:T(8,128)} %reduce-scatter.5.cloned.1.call-done), channel_id=3, replica_groups=mesh['dp'=64,'mp'=4] {'dp'}, use_global_device_ids=true, to_apply=%region_5.6.clone | all-reduce | flops 425984 | bytes 2555904
  (83 shorter events, 43.1 us)
Async XLA Ops:
  7.2 36.3 %copy-start = (bf16[40,6656]{1,0:T(8,128)(2,1)S(1)}, bf16[40,6656]{1,0:T(8,128)(2,1)}, u32[]{:S(2)}) copy-start(bf16[40,6656]{1,0:T(8,128)(2,1)} %param.11) | copy-start | bytes 1597444
  9.0 26.0 %all-to-all-start = ((s32[256,1,30]{2,1,0:T(1,128)}), s32[256,1,30]{2,1,0:T(1,128)S(1)}, u32[]{:S(2)}, u32[]{:S(2)}) async-start(s32[256,1,30]{2,1,0:T(1,128)} %stack.4), calls=%async_computation | async-start | bytes 262144 | tf_op jit(solution)/shard_map/all_to_all | solution.py:45
  49.5 5.7 copy-start.2
  49.5 85.1 %all-to-all-start.3 = ((bf16[64,3,6656]{2,1,0:T(4,128)(2,1)}), bf16[64,3,6656]{2,1,0:T(4,128)(2,1)}, u32[]{:S(2)}, u32[]{:S(2)}) async-start(bf16[64,3,6656]{2,1,0:T(4,128)(2,1)} %all_to_all.35), calls=%async_computation.3 | async-start | bytes 6815744 | tf_op jit(solution)/shard_map/all_to_all | solution.py:84
  61.3 79.0 %copy-start.8 = (bf16[2,1664]{1,0:T(2,128)(2,1)S(1)}, bf16[2,1664]{1,0:T(2,128)(2,1)}, u32[]{:S(2)}) copy-start(bf16[2,1664]{1,0:T(2,128)(2,1)} %param.7) | copy-start | bytes 19972
  61.3 91.6 %copy-start.3 = (bf16[40,6656]{1,0:T(8,128)(2,1)S(1)}, bf16[40,6656]{1,0:T(8,128)(2,1)}, u32[]{:S(2)}) copy-start(bf16[40,6656]{1,0:T(8,128)(2,1)} %param.9) | copy-start | bytes 1597444
  134.6 87.2 %all-to-all-start.2 = ((bf16[64,3,6656]{2,1,0:T(4,128)(2,1)}), bf16[64,3,6656]{2,1,0:T(4,128)(2,1)}, u32[]{:S(2)}, u32[]{:S(2)}) async-start(bf16[64,3,6656]{2,1,0:T(4,128)(2,1)} %all_to_all.32), calls=%async_computation.2 | async-start | bytes 6815744 | tf_op jit(solution)/shard_map/all_to_all | solution.py:83
  140.2 191.3 %all-gather.5.cloned.1.call-start = ((), (), s32[]{:S(2)}) async-start(), calls=%async_computation.8 | async-start | bytes 1730560 | tf_op jit(solution)/shard_map/all_gather | solution.py:78
  159.0 68.8 %copy-start.9 = (bf16[2,1664]{1,0:T(2,128)(2,1)S(1)}, bf16[2,1664]{1,0:T(2,128)(2,1)}, u32[]{:S(2)}) copy-start(bf16[2,1664]{1,0:T(2,128)(2,1)} %param.8) | copy-start | bytes 19972
  221.9 141.7 %all-to-all-start.1 = ((bf16[64,3,6656]{2,1,0:T(4,128)(2,1)}), bf16[64,3,6656]{2,1,0:T(4,128)(2,1)}, u32[]{:S(2)}, u32[]{:S(2)}) async-start(bf16[64,3,6656]{2,1,0:T(4,128)(2,1)} %all_to_all.29), calls=%async_computation.1 | async-start | bytes 6815744 | tf_op jit(solution)/shard_map/all_to_all | solution.py:82
  227.8 107.7 %all-gather.7.cloned.1.call-start = ((), (), s32[]{:S(2)}) async-start(), calls=%async_computation.9 | async-start | bytes 1730560 | tf_op jit(solution)/shard_map/all_gather | solution.py:79
  240.4 184.2 %reduce-scatter.5.cloned.1.call-start = ((), (), s32[]{:S(2)}) async-start(), calls=%async_computation.7 | async-start | bytes 4259840 | tf_op jit(solution)/shard_map/reduce_scatter | solution.py:94
  244.5 87.1 %copy-start.10 = (s32[60]{0:T(128)S(1)}, s32[60]{0:T(128)}, u32[]{:S(2)}) copy-start(s32[60]{0:T(128)} %param.13) | copy-start | bytes 724
  374.3 2.7 copy-start.4
  374.3 2.7 copy-start.5
  377.8 1.2 copy-start.7
  381.3 1.2 copy-start.6
  381.3 88.4 %reduce-scatter.3.cloned.1.call-start = ((), (), s32[]{:S(2)}) async-start(), calls=%async_computation.6 | async-start | bytes 4259840 | tf_op jit(solution)/shard_map/reduce_scatter | solution.py:93
  384.9 0.7 copy-start.11
  389.5 350.2 %copy-start.1 = (bf16[40,6656]{1,0:T(8,128)(2,1)S(1)}, bf16[40,6656]{1,0:T(8,128)(2,1)}, u32[]{:S(2)}) copy-start(bf16[40,6656]{1,0:T(8,128)(2,1)} %param.11) | copy-start | bytes 1597444
Sparse Core Ops, SparseCore 0:
  153.1 84.7 all-gather.4
  240.6 85.1 all-gather.6
  381.5 43.0 reduce-scatter.4
  427.0 42.6 reduce-scatter.2
